TPU v7x, 512 devices: a whole 4x4x16 slice. The times are simulated.
512 devices in a mesh: dp: 32 (over z_hi, y, x), tensor: 16 (over z_lo, core).
Axes of the slice: x: 4, y: 4, z: 16 (z_hi: 2, z_lo: 8; z = z_hi * 8 + z_lo), core: 2. Of those that a mesh axis runs over, the one named last changes fastest.
Arguments:
- resid_src: bfloat16 [256, 4608], P('dp', 'tensor'), may hold values from -6 to 6
- enc_weight: bfloat16 [4608, 131072], P(None, ('dp', 'tensor')), may hold values from -0.09375 to 0.09375
- enc_bias: float32 [131072], P(('dp', 'tensor')), may hold values from -3 to 3
- active_ids: int32 [256, 64], replicated, may hold values from -1 to 131071, as said below
- dec_weight: bfloat16 [131072, 4608], P('dp', 'tensor'), may hold values from -0.75 to 0.75
- dec_bias: float32 [4608], P('tensor'), may hold values from -3 to 3
- segments: int32 [256], replicated, may hold values from 0 to 3, never falling along the last dimension, each value on 1 to 128 neighbouring positions
- attn_in_gain: float32 [4608], replicated, may hold values from 0.25 to 1.75
- post_gain: float32 [4608], replicated, may hold values from 0.25 to 1.75
- q_weight: bfloat16 [4608, 4096], P('dp', 'tensor'), may hold values from -1.41421356 to 1.41421356
- k_weight: bfloat16 [4608, 2048], P('dp', 'tensor'), may hold values from -0.09375 to 0.09375
- v_weight: bfloat16 [4608, 2048], P('dp', 'tensor'), may hold values from -0.09375 to 0.09375
- o_weight: bfloat16 [4096, 4608], P('tensor', 'dp'), may hold values from -0.09375 to 0.09375
Outputs:
- block_out: bfloat16 [256, 4608], P('dp', 'tensor')
Inputs may be any that keep to these rules, and one draw needn't show every extreme that they name: `active_ids`: each row holds a number of latent ids, at least 32 and at most 64, followed by -1 in the remaining slots; ids may repeat within a row.
All inputs are finite; a program needn't handle non-finite values.
Results may differ from a plain program's by a relative error of at most 0.012.
The roundings to bfloat16 on the way count: a program that leaves them out, or rounds other values in their place, can miss the bound.
Values may be sent and summed in bfloat16 or wider, within the bound.
A program may use at most 64 MiB of HBM per device.

v0:
```python
import math

import jax
import jax.numpy as jnp
from jax import lax
from jax.sharding import PartitionSpec as P

QUERY_SCALE = 144.0 ** (-0.5)
SOFT_CAP = 50.0


def norm_rows(values, gain):
    return values * lax.rsqrt(jnp.mean(values * values, axis=-1, keepdims=True) + 1e-06) * gain


def rotate(heads_in, positions):
    half_dim = heads_in.shape[-1] // 2
    freq_index = jnp.arange(half_dim, dtype=jnp.float32)
    inverse = jnp.exp(freq_index * (-2.0 * math.log(10000.0) / heads_in.shape[-1]))
    angles = positions[:, None, None] * inverse[None, None, :]
    cosine = jnp.cos(angles)
    sine = jnp.sin(angles)
    first = heads_in[..., :half_dim]
    second = heads_in[..., half_dim:]
    return jnp.concatenate(
        [first * cosine - second * sine, second * cosine + first * sine], axis=-1
    )


def local(
    resid_src,
    enc_weight,
    enc_bias,
    active_ids,
    dec_weight,
    dec_bias,
    segments,
    attn_in_gain,
    post_gain,
    q_weight,
    k_weight,
    v_weight,
    o_weight,
):
    tok_local = resid_src.shape[0]
    all_tokens = segments.shape[0]
    head_size = k_weight.shape[1]
    query_cols = q_weight.shape[1]
    heads_here = query_cols // head_size
    features = lax.all_gather(resid_src, "tensor", axis=1, tiled=True)
    pre_act = (
        jnp.dot(
            lax.all_gather(features, "dp", axis=0, tiled=True),
            enc_weight,
            preferred_element_type=jnp.float32,
        )
        + enc_bias
    )
    latent_act = jnp.maximum(pre_act, 0.0).astype(jnp.bfloat16)
    own_width = latent_act.shape[1]
    group_width = own_width * lax.axis_size("tensor")
    group_base = lax.axis_index("dp") * group_width
    relative = active_ids - group_base
    inside = (active_ids >= 0) & (relative >= 0) & (relative < group_width)
    col_ids = jnp.where(inside, relative, group_width)
    row_ids = jnp.broadcast_to(jnp.arange(all_tokens, dtype=jnp.int32)[:, None], active_ids.shape)
    group_act = lax.all_gather(latent_act, "tensor", axis=1, tiled=True)
    counts = (
        jnp.zeros((all_tokens, group_width), jnp.float32)
        .at[row_ids, col_ids]
        .add(inside.astype(jnp.float32), mode="drop")
    )
    selected = group_act * counts.astype(jnp.bfloat16)
    rows = selected
    recon = lax.psum_scatter(
        jnp.dot(rows, dec_weight, preferred_element_type=jnp.float32),
        "dp",
        scatter_dimension=0,
        tiled=True,
    )
    spliced = (recon + dec_bias).astype(jnp.bfloat16)
    full_rows = lax.all_gather(spliced, "tensor", axis=1, tiled=True)
    normed = norm_rows(full_rows.astype(jnp.float32), attn_in_gain).astype(jnp.bfloat16)
    rows = normed
    query_lin = jnp.dot(
        rows, lax.all_gather(q_weight, "dp", axis=0, tiled=True), preferred_element_type=jnp.float32
    )
    key_lin = jnp.dot(
        rows, lax.all_gather(k_weight, "dp", axis=0, tiled=True), preferred_element_type=jnp.float32
    )
    value_lin = jnp.dot(
        rows, lax.all_gather(v_weight, "dp", axis=0, tiled=True), preferred_element_type=jnp.float32
    )
    query_start = lax.axis_index("dp") * tok_local
    query_index = query_start + jnp.arange(tok_local, dtype=jnp.int32)
    query_docs = lax.dynamic_slice_in_dim(segments, query_start, tok_local, 0)
    every_index = jnp.arange(all_tokens, dtype=jnp.int32)
    same_doc = query_docs[:, None] == segments[None, :]
    positions = jnp.sum(same_doc & (every_index[None, :] < query_index[:, None]), axis=1).astype(
        jnp.float32
    )
    queries = (
        rotate(query_lin.reshape(tok_local, heads_here, head_size), positions) * QUERY_SCALE
    ).astype(jnp.bfloat16)
    key_rows = rotate(key_lin.reshape(tok_local, 1, head_size), positions)[:, 0].astype(
        jnp.bfloat16
    )
    value_rows = value_lin.astype(jnp.bfloat16)
    key_piece = lax.all_gather(key_rows, "dp", axis=0, tiled=True)
    value_piece = lax.all_gather(value_rows, "dp", axis=0, tiled=True)
    width = key_piece.shape[0]
    key_index = jnp.arange(width, dtype=jnp.int32)
    scores = jnp.einsum("qhd,kd->hqk", queries, key_piece, preferred_element_type=jnp.float32)
    capped = SOFT_CAP * jnp.tanh(scores / SOFT_CAP)
    allowed = (query_docs[:, None] == segments[None, :]) & (
        key_index[None, :] <= query_index[:, None]
    )
    weights = jnp.where(allowed[None], jnp.exp(capped), 0.0)
    mixed = jnp.einsum(
        "hqk,kd->hqd", weights.astype(jnp.bfloat16), value_piece, preferred_element_type=jnp.float32
    )
    totals = jnp.sum(weights, axis=-1)
    heads_out = (
        (mixed / totals[:, :, None])
        .transpose(1, 0, 2)
        .reshape(tok_local, query_cols)
        .astype(jnp.bfloat16)
    )
    partial_value = jnp.dot(
        heads_out,
        lax.all_gather(o_weight, "dp", axis=1, tiled=True),
        preferred_element_type=jnp.float32,
    )
    share_width = spliced.shape[1]
    share_start = lax.axis_index("tensor") * share_width
    attended = lax.psum(partial_value, "tensor")
    post_share = lax.dynamic_slice_in_dim(
        norm_rows(attended, post_gain), share_start, share_width, 1
    )
    return (spliced.astype(jnp.float32) + post_share).astype(jnp.bfloat16)


def solution(mesh):
    return jax.shard_map(
        local,
        mesh=mesh,
        in_specs=(
            P("dp", "tensor"),
            P(None, ("dp", "tensor")),
            P(("dp", "tensor")),
            P(),
            P("dp", "tensor"),
            P("tensor"),
            P(),
            P(),
            P(),
            P("dp", "tensor"),
            P("dp", "tensor"),
            P("dp", "tensor"),
            P("tensor", "dp"),
        ),
        out_specs=P("dp", "tensor"),
        check_vma=False,
    )
```

profile of v0, /device:TPU:1, one launch (start us, length us, event | category | flops | bytes accessed | tf_op | source)
XLA Modules:
  0.0 1508.2 jit_solution(10807216923978818210)
XLA Ops:
  6.5 0.0 copy-start
  6.5 0.0 all-gather.10.cloned.1.call-start
  6.5 38.2 %all-gather.1 = bf16[16,288,8]{1,2,0:T(8,128)(2,1)S(1)} all-gather(bf16[1,288,8]{1,2,0:T(8,128)(2,1)} %bitcast.60), channel_id=1, replica_groups=mesh['dp'=32,'tensor'=16] {'tensor'}, dimensions={0}, use_global_device_ids=true | all-gather | bytes 78336 | tf_op jit(solution)/shard_map/all_gather | solution.py:50
  44.8 0.8 reshape.220
  45.5 0.0 all-gather.10.cloned.1.call-update
  45.6 0.0 copy-start.1
  45.6 0.0 copy-start.6
  45.6 0.0 copy-start.5
  45.6 0.0 all-gather.12.cloned.1.call-start
  45.6 131.2 %all-gather.10.cloned.1.call-done = bf16[256,4608]{1,0:T(8,128)(2,1)} async-done(((bf16[8,4608]{1,0:T(8,128)(2,1)}), bf16[256,4608]{1,0:T(8,128)(2,1)}) %all-gather.10.cloned.1.call-update) | async-done | bytes 2359312 | tf_op jit(solution)/shard_map/all_gather | solution.py:53
  176.9 3.8 fusion.5
  180.7 0.0 all-gather.12.cloned.1.call-update
  180.7 0.0 all-reduce.6.cloned.1.call-start
  180.8 0.1 multiply_reduce_fusion.2
  180.9 0.0 copy-done.5
  180.9 0.1 and_reduce_fusion
  181.0 0.1 copy.18
  181.1 0.1 reshape.212
  181.3 0.1 copy.19
  181.4 0.1 reshape.214
  181.4 88.0 %scatter_custom_fusion = f32[1048576]{0:T(1024)} fusion(s32[16384]{0:T(1024)S(1)} %reshape.212, f32[16384]{0:T(1024)S(1)} %reshape.214, f32[]{:T(128)} %constant.16.clone.1), kind=kCustom, calls=%fused_computation.1 | custom fusion | flops 16384 | bytes 4194308
  269.4 3.7 convert_element_type.69
  273.2 4.2 reshape.211
  277.3 0.0 all-gather.12.cloned.1.call-done
  277.4 4.2 fusion.2
  281.6 0.0 all-reduce.6.cloned.1.call-update
  281.6 0.0 all-gather.14.cloned.1.call-start
  281.7 0.5 all-gather.14.cloned.1.call-update
  282.2 0.0 all-gather.18.cloned.1.call-start
  282.3 0.5 all-gather.18.cloned.1.call-update
  282.8 0.0 all-gather.16.cloned.1.call-start
  282.9 0.5 all-gather.16.cloned.1.call-update
  283.4 0.0 all-gather.20.cloned.1.call-start
  283.4 0.7 all-gather.20.cloned.1.call-update
  284.1 0.0 all-reduce.4.cloned.1.call-start
  284.2 0.1 dynamic_slice.6
  284.3 0.2 convert_reduce_fusion
  284.5 1.3 dynamic-slice
  286.4 0.1 compare_and_fusion.2
  286.5 0.1 multiply_cosine_fusion
  286.6 529.9 %all-reduce.6.cloned.1.call-done = f32[256,288]{1,0:T(8,128)} async-done(((f32[256,288]{1,0:T(8,128)}), f32[256,288]{1,0:T(8,128)}) %all-reduce.6.cloned.1.call-update) | async-done | bytes 294928
  816.5 0.7 fusion.38
  817.2 53.3 %all-gather.2 = bf16[16,288,8]{1,2,0:T(8,128)(2,1)S(1)} all-gather(bf16[1,288,8]{1,2,0:T(8,128)(2,1)S(1)} %fusion.38), channel_id=1, replica_groups=mesh['dp'=32,'tensor'=16] {'tensor'}, dimensions={0}, use_global_device_ids=true | all-gather | bytes 78336 | tf_op jit(solution)/shard_map/all_gather | solution.py:82
  870.5 0.1 reshape.223
  870.6 0.2 multiply_reduce_fusion
  870.8 0.0 copy-done.2
  870.8 0.1 multiply_convert_fusion
  870.9 79.3 %all-gather.14.cloned.1.call-done = bf16[4608,128]{1,0:T(8,128)(2,1)} async-done(((bf16[144,128]{1,0:T(8,128)(2,1)}), bf16[4608,128]{1,0:T(8,128)(2,1)}) %all-gather.14.cloned.1.call-update) | async-done | bytes 1179664 | tf_op jit(solution)/shard_map/all_gather | solution.py:89
  950.2 1.5 convolution_bitcast_fusion.2
  951.7 0.1 fusion.32
  951.8 0.1 pad_maximum_fusion
  951.9 135.2 %all-gather = bf16[256,1,128]{2,0,1:T(8,128)(2,1)S(1)} all-gather(bf16[8,1,128]{2,0,1:T(8,128)(2,1)S(1)} %pad_maximum_fusion), channel_id=2, replica_groups=mesh['dp'=32,'tensor'=16] {'dp'}, dimensions={0}, use_global_device_ids=true | all-gather | bytes 67584 | tf_op jit(solution)/shard_map/all_gather | solution.py:109
  1087.1 1.5 convolution_convert_fusion
  1088.6 142.2 %all_gather.38 = bf16[256,128]{1,0:T(8,128)(2,1)S(1)} all-gather(bf16[8,128]{1,0:T(8,128)(2,1)S(1)} %convolution_convert_fusion), channel_id=1, replica_groups=mesh['dp'=32,'tensor'=16] {'dp'}, dimensions={0}, use_global_device_ids=true | all-gather | bytes 67584 | tf_op jit(solution)/shard_map/all_gather | solution.py:110
  1230.8 2.1 convolution_bitcast_fusion.1
  1232.9 0.1 multiply_subtract_fusion
  1233.0 0.3 fusion.41
  1233.3 85.6 %all-gather.20.cloned.1.call-done = bf16[256,4608]{0,1:T(8,128)(2,1)} async-done(((bf16[256,144]{0,1:T(8,128)(2,1)}), bf16[256,4608]{0,1:T(8,128)(2,1)}) %all-gather.20.cloned.1.call-update) | async-done | bytes 2359312 | tf_op jit(solution)/shard_map/all_gather | solution.py:131
  1318.9 3.1 fusion.14
  1322.0 0.0 all-reduce.4.cloned.1.call-update
  1322.0 0.8 dynamic-slice.2
  1322.8 176.1 %all-reduce.4.cloned.1.call-done = f32[8,4608]{1,0:T(8,128)} async-done(((f32[8,4608]{1,0:T(8,128)}), f32[8,4608]{1,0:T(8,128)}) %all-reduce.4.cloned.1.call-update) | async-done | bytes 147472 | tf_op jit(solution)/shard_map/psum | solution.py:136
  1498.9 1.1 multiply_reduce_fusion.1
  1500.0 1.4 fusion.21
  (21 shorter events, 0.1 us)
Async XLA Ops:
  6.5 270.8 %copy-start = (bf16[4096,288]{0,1:T(8,128)(2,1)S(1)}, bf16[4096,288]{0,1:T(8,128)(2,1)}, u32[]{:S(2)}) copy-start(bf16[4096,288]{0,1:T(8,128)(2,1)} %param.17) | copy-start | bytes 7077892
  6.5 170.3 %all-gather.10.cloned.1.call-start = ((), (), s32[]{:S(2)}) async-start(), calls=%async_computation | async-start | bytes 2433024 | tf_op jit(solution)/shard_map/all_gather | solution.py:53
  45.6 135.2 %copy-start.1 = (s32[256,64]{0,1:T(8,128)S(1)}, s32[256,64]{0,1:T(8,128)}, u32[]{:S(2)}) copy-start(s32[256,64]{0,1:T(8,128)} %param.16) | copy-start | bytes 196612
  45.6 135.2 %copy-start.6 = (s32[2]{0:T(128)S(1)}, s32[2]{0:T(128)}, u32[]{:S(2)}) copy-start(s32[2]{0:T(128)} %constant.50) | copy-start | bytes 28
  45.6 135.3 %copy-start.5 = (s32[2]{0:T(128)S(1)}, s32[2]{0:T(128)}, u32[]{:S(2)}) copy-start(s32[2]{0:T(128)} %constant.53) | copy-start | bytes 28
  45.6 231.8 %all-gather.12.cloned.1.call-start = ((), (), s32[]{:S(2)}) async-start(), calls=%async_computation.1 | async-start | bytes 2228224 | tf_op jit(solution)/shard_map/all_gather | solution.py:67
  180.7 635.8 %all-reduce.6.cloned.1.call-start = ((), (), s32[]{:S(2)}) async-start(), calls=%async_computation.7 | async-start | bytes 786432
  277.3 6.9 copy-start.4
  277.3 539.1 %copy-start.3 = (f32[288]{0:T(512)S(1)}, f32[288]{0:T(512)}, u32[]{:S(2)}) copy-start(f32[288]{0:T(512)} %param.18) | copy-start | bytes 3460
  277.3 593.5 %copy-start.2 = (f32[4608]{0:T(1024)S(1)}, f32[4608]{0:T(1024)}, u32[]{:S(2)}) copy-start(f32[4608]{0:T(1024)} %param.20) | copy-start | bytes 55300
  281.6 668.6 %all-gather.14.cloned.1.call-start = ((), (), s32[]{:S(2)}) async-start(), calls=%async_computation.2 | async-start | bytes 1216512 | tf_op jit(solution)/shard_map/all_gather | solution.py:89
  282.2 804.9 %all-gather.18.cloned.1.call-start = ((), (), s32[]{:S(2)}) async-start(), calls=%async_computation.4 | async-start | bytes 1216512 | tf_op jit(solution)/shard_map/all_gather | solution.py:92
  282.8 948.0 %all-gather.16.cloned.1.call-start = ((), (), s32[]{:S(2)}) async-start(), calls=%async_computation.3 | async-start | bytes 2433024 | tf_op jit(solution)/shard_map/all_gather | solution.py:86
  283.4 1035.5 %all-gather.20.cloned.1.call-start = ((), (), s32[]{:S(2)}) async-start(), calls=%async_computation.5 | async-start | bytes 2433024 | tf_op jit(solution)/shard_map/all_gather | solution.py:131
  284.1 1214.8 %all-reduce.4.cloned.1.call-start = ((), (), s32[]{:S(2)}) async-start(), calls=%async_computation.6 | async-start | bytes 294912 | tf_op jit(solution)/shard_map/psum | solution.py:136
Sparse Core Ops, SparseCore 0:
  45.7 131.1 all-gather.9
  180.8 74.7 all-gather.11
  281.8 534.6 all-reduce.5
  821.3 128.8 all-gather.13
  955.0 103.0 all-gather.17
  1063.0 125.6 all-gather.15
  1193.7 125.1 all-gather.19
  1322.1 176.7 all-reduce.3
where the time goes:
time: 1510 us
  waiting for transfers between devices  1000 us (66%)
  blocking collectives  369 us (24%)
  other arithmetic  96 us (6%)
  matrix products  16.6 us (1%)
    unnamed x9, waiting for transfers between devices  532 us
    psum x1, waiting for transfers between devices, local(): attended = lax.psum(partial_value, 'tensor')  176 us
    all_gather x1, blocking collectives, local(): value_piece = lax.all_gather(value_rows, 'dp', axis=0, tiled=True)  142 us
    all_gather x1, blocking collectives, local(): key_piece = lax.all_gather(key_rows, 'dp', axis=0, tiled=True)  135 us
    all_gather x1, waiting for transfers between devices, local(): lax.all_gather(features, 'dp', axis=0, tiled=True)  131 us
    unnamed x5, other arithmetic  88.9 us
    all_gather x1, waiting for transfers between devices, local(): lax.all_gather(o_weight, 'dp', axis=1, tiled=True)  85.6 us
    all_gather x1, waiting for transfers between devices, local(): lax.all_gather(k_weight, 'dp', axis=0, tiled=True)  79.3 us
  transfers between devices with their start and end apart: 8, of which 5 were waited for; matrix products, arithmetic and copies ran while one was open for 7% of the time, Pallas kernels for 0%

commit v1 on v0

v1 whole, which is shorter than its diff:
```python
import math

import jax
import jax.numpy as jnp
from jax import lax
from jax.experimental import pallas as pl
from jax.experimental.pallas import tpu as pltpu
from jax.sharding import PartitionSpec as P

QUERY_SCALE = 144.0 ** (-0.5)
SOFT_CAP = 50.0
EPS = 1e-06
MESH = pl.DeviceIdType.MESH
F32 = jnp.float32
BF16 = jnp.bfloat16


def kernel(
    NP, NT,
    resid, enc_hbm, enc_bias, ids_ref, dec_hbm, dec_bias, segs, gain_in, gain_post,
    q_hbm, k_hbm, v_hbm, o_hbm,
    out_ref,
    E, DEC, WQ, WK, WV, WO,
    COL, X, IDP, B, VS, VR, VG, S,
    RS, RR, ZS, ZR, SPF, SP, GIN, GPO, XS, XR, PS, PR, YS, YR, QR,
    CT, ST, MASK, HO, OS, OR, AS, AR, NR,
    lsem, ssem, rsem, r1b, r1c,
):
    T = 16 * NP
    R8 = 8 * NP
    NZ = NT // 2
    CH = resid.shape[1]
    HC = CH // 2
    D = NT * CH
    g = lax.axis_index("dp")
    s = lax.axis_index("tensor")
    zh = g // NP
    p = g % NP
    zl = s // 2
    c = s % 2

    def rcopy(src, dst, k, dp, tensor, rs=None):
        return pltpu.make_async_remote_copy(
            src_ref=src, dst_ref=dst, send_sem=ssem.at[k],
            recv_sem=rsem.at[k] if rs is None else rs,
            device_id={"dp": dp, "tensor": tensor}, device_id_type=MESH)

    def bulk(ref, n, sem):
        d = ref.at[pl.ds(0, n)]
        pltpu.make_async_copy(d, d, sem).wait()

    def to_plane(k, src, dst, rs=None):
        @pl.loop(1, NP)
        def _(j):
            q = (p + j) % NP
            rcopy(src(q), dst, k, zh * NP + q, s, rs).start()

    def to_tensor(k, src, dst):
        @pl.loop(1, NT)
        def _(j):
            q = (s + j) % NT
            rcopy(src(q), dst, k, g, q).start()

    loads = []
    for z in range(NZ):
        for h in range(2):
            row = pl.multiple_of((2 * z + (c if h == 0 else 1 - c)) * CH, 16)
            loads.append(pltpu.make_async_copy(
                enc_hbm.at[pl.ds(row, CH)], E.at[h, pl.ds(z * CH, CH)], lsem.at[len(loads)]))
    n_enc = len(loads)
    for a, b in ((dec_hbm, DEC), (q_hbm, WQ), (k_hbm, WK), (v_hbm, WV), (o_hbm, WO)):
        loads.append(pltpu.make_async_copy(a, b, lsem.at[len(loads)]))

    me_z = zh * NZ + zl
    @pl.loop(1, 2 * NZ)
    def _(j):
        z = (me_z + j) % (2 * NZ)
        rcopy(resid, COL.at[me_z], 0, (z // NZ) * NP + p, (z % NZ) * 2 + c).start()
    COL[me_z] = resid[...]
    for cp in loads:
        cp.start()

    a = ids_ref[...]
    IDP[:, :64] = a[:R8]
    IDP[:, 64:] = a[R8:]
    for j in range(NT):
        GIN[j:j + 1, :] = gain_in[:, j * CH:(j + 1) * CH]
        GPO[j:j + 1, :] = gain_post[:, j * CH:(j + 1) * CH]

    bulk(COL, 2 * NZ - 1, rsem.at[0])
    halves = []
    for h in range(2):
        halves.append(jnp.concatenate(
            [COL[h * NZ + z].astype(F32) for z in range(NZ)], axis=1))
    X[0, p] = jnp.concatenate(halves, axis=0).astype(BF16)
    to_plane(1, lambda q: X.at[0, p], X.at[0, p], r1b.at[p])
    rcopy(X.at[0, p], X.at[1, p], 2, g, s + 1 - 2 * c, r1c.at[p]).start()

    def tok(r):
        return ((r // 8) % 2) * R8 + (r // 16) * 8 + r % 8
    segc = jnp.broadcast_to(segs[...].astype(F32), (T, T)).T
    segc = jnp.concatenate(
        [segc[h * R8 + b * 8:h * R8 + b * 8 + 8] for b in range(NP) for h in range(2)], axis=0)
    tr = tok(lax.broadcasted_iota(jnp.int32, (T, T), 0))
    tc = tok(lax.broadcasted_iota(jnp.int32, (T, T), 1))
    same = segc == segc.T
    MASK[...] = jnp.where(same & (tc <= tr), 1.0, 0.0)
    pos = jnp.sum(jnp.where(same & (tc < tr), 1.0, 0.0), axis=1, keepdims=True)
    lane = lax.broadcasted_iota(jnp.int32, (1, 128), 1)
    inverse = jnp.exp((lane % 64).astype(F32) * (-2.0 * math.log(10000.0) / 128))
    ang = pos * inverse
    CT[...] = jnp.cos(ang)
    ST[...] = jnp.where(lane < 64, -1.0, 1.0) * jnp.sin(ang)

    def onehot(b):
        lo = (IDP[pl.ds(pl.multiple_of(b * 8, 8), 8), :] & 255).astype(F32).T
        cols = lax.broadcasted_iota(jnp.int32, (128, 256), 1).astype(F32)
        for i in range(8):
            B[b, pl.ds(i * 128, 128), :] = jnp.where(lo[:, i:i + 1] == cols, 1.0, 0.0).astype(BF16)

    onehot(0)
    @pl.loop(1, NP)
    def _(j):
        onehot(j)
        q = (p + NP - j) % NP
        pltpu.make_async_copy(X.at[0, q], X.at[0, q], r1b.at[q]).wait()
        rcopy(X.at[0, q], X.at[1, q], 2, g, s + 1 - 2 * c, r1c.at[q]).start()

    for cp in loads[:n_enc]:
        cp.wait()
    pre = jnp.dot(X[0].reshape(T, NZ * CH), E[0], preferred_element_type=F32)
    @pl.loop(0, NP)
    def _(q):
        pltpu.make_async_copy(X.at[1, q], X.at[1, q], r1c.at[q]).wait()
    pre = pre + jnp.dot(X[1].reshape(T, NZ * CH), E[1], preferred_element_type=F32)
    act = jnp.maximum(pre + enc_bias[...], 0.0).astype(BF16).astype(F32)

    act = act.reshape(NP, 2, 8, 256)
    a0 = act[:, 0].reshape(R8, 256)
    a1 = act[:, 1].reshape(R8, 256)
    rel = IDP[...] - (g * NT + s) * 256
    low = rel & 127
    left = lax.broadcasted_iota(jnp.int32, (R8, 128), 1) < 64

    def pick(h):
        return jnp.where(
            left,
            jnp.take_along_axis(a0[:, h * 128:(h + 1) * 128], low, axis=1),
            jnp.take_along_axis(a1[:, h * 128:(h + 1) * 128], low, axis=1))
    val = jnp.where(rel >= 128, pick(1), pick(0))
    val = jnp.where((rel >= 0) & (rel < 256), val, 0.0)
    VS[...] = val.reshape(NT, 8, 128)
    VR[s] = VS[s]
    to_tensor(3, lambda q: VS.at[q], VR.at[s])
    bulk(VR, NT - 1, rsem.at[3])
    VG[s] = jnp.sum(VR[...], axis=0)
    to_tensor(4, lambda q: VG.at[s], VG.at[s])
    bulk(VG, NT - 1, rsem.at[4])

    sub = lax.broadcasted_iota(jnp.int32, (8, 128), 0)
    lft = lax.broadcasted_iota(jnp.int32, (8, 128), 1) < 64
    @pl.loop(0, NP)
    def _(b):
        relb = IDP[pl.ds(pl.multiple_of(b * 8, 8), 8), :] - g * (NT * 256)
        vb = VG[b]
        hi = jnp.where(relb < 0, -1, relb >> 8)
        v0 = jnp.where(lft, vb, 0.0)
        v1 = vb - v0
        rows = []
        for h in range(NT):
            for vz in (v0, v1):
                d = jnp.where(hi == h, vz, 0.0)
                rows.append(jnp.concatenate([jnp.where(sub == i, d, 0.0) for i in range(8)], axis=1))
        lhs = jnp.concatenate(rows, axis=0).astype(BF16)
        sel = jnp.dot(lhs, B[b], preferred_element_type=F32).astype(BF16)
        S[:, pl.ds(pl.multiple_of(b * 16, 16), 16), :] = sel.reshape(NT, 16, 256)
    loads[n_enc].wait()
    rec = jnp.dot(S[0], DEC[pl.ds(0, 256), :], preferred_element_type=F32)
    for h in range(1, NT):
        rec = rec + jnp.dot(S[h], DEC[pl.ds(h * 256, 256), :], preferred_element_type=F32)
    RS[...] = rec.reshape(NP, 16, CH)
    RR[p] = RS[p]
    to_plane(5, lambda q: RS.at[q], RR.at[p])
    bulk(RR, NP - 1, rsem.at[5])
    ZS[...] = jnp.sum(RR[...], axis=0)
    zp = (1 - zh) * NP + p
    zc = rcopy(ZS, ZR, 6, zp, s)
    zc.start()
    zc.wait_recv()
    spl = (ZS[...] + ZR[...] + dec_bias[...]).astype(BF16)
    SPF[...] = spl.astype(F32).reshape(2, 8, CH)
    SP[s] = spl
    to_tensor(7, lambda q: SP.at[s], SP.at[s])
    for cp in loads[n_enc + 1:]:
        cp.wait()
    bulk(SP, NT - 1, rsem.at[7])

    ss = jnp.zeros((16, 1), F32)
    for j in range(NT):
        xj = SP[j].astype(F32)
        ss = ss + jnp.sum(xj * xj, axis=1, keepdims=True)
    rn = lax.rsqrt(ss / D + EPS)
    for j in range(NP // 2):
        cj = zh * (NP // 2) + j
        n = SP[cj].astype(F32) * rn * GIN[pl.ds(cj, 1), :]
        XS[2 * j] = n[:, :HC].astype(BF16)
        XS[2 * j + 1] = n[:, HC:].astype(BF16)
    XR[p] = XS[p]
    to_plane(8, lambda q: XS.at[q], XR.at[p])
    bulk(XR, NP - 1, rsem.at[8])
    xr = XR[...].reshape(T, HC)
    PS[:, :, 0:256] = jnp.dot(xr, WQ[...], preferred_element_type=F32).reshape(NP, 16, 256)
    PS[:, :, 256:384] = jnp.dot(xr, WK[...], preferred_element_type=F32).reshape(NP, 16, 128)
    PS[:, :, 384:512] = jnp.dot(xr, WV[...], preferred_element_type=F32).reshape(NP, 16, 128)
    PR[p] = PS[p]
    to_plane(9, lambda q: PS.at[q], PR.at[p])
    bulk(PR, NP - 1, rsem.at[9])
    YS[...] = jnp.sum(PR[...], axis=0)
    yc = rcopy(YS, YR, 10, zp, s)
    yc.start()
    yc.wait_recv()
    y = YS[...] + YR[...]
    mine = pl.ds(pl.multiple_of(p * 16, 16), 16)
    cosine, sine = CT[mine, :], ST[mine, :]

    def rot(x):
        return x * cosine + pltpu.roll(x, 64, 1) * sine
    QR[p] = jnp.concatenate(
        [rot(y[:, 0:128]) * QUERY_SCALE, rot(y[:, 128:256]) * QUERY_SCALE,
         rot(y[:, 256:384]), y[:, 384:512]], axis=1).astype(BF16)
    to_plane(11, lambda q: QR.at[p], QR.at[p])
    bulk(QR, NP - 1, rsem.at[11])

    kk = QR[:, :, 256:384].reshape(T, 128)
    vv = QR[:, :, 384:512].reshape(T, 128)
    for h in range(2):
        qq = QR[:, :, h * 128:(h + 1) * 128].reshape(T, 128)
        sc = lax.dot_general(qq, kk, (((1,), (1,)), ((), ())), preferred_element_type=F32)
        w = jnp.where(MASK[...] > 0.0, jnp.exp(SOFT_CAP * jnp.tanh(sc / SOFT_CAP)), 0.0)
        tot = jnp.sum(w, axis=1, keepdims=True)
        mixed = jnp.dot(w.astype(BF16), vv, preferred_element_type=F32)
        HO[:, h * 128:(h + 1) * 128] = (mixed / tot).astype(BF16)
    OS[...] = jnp.dot(HO[...], WO[...], preferred_element_type=F32).reshape(NT, 16, HC)
    OR[s] = OS[s]
    to_tensor(12, lambda q: OS.at[q], OR.at[s])
    bulk(OR, NT - 1, rsem.at[12])
    AS[...] = jnp.sum(OR[...], axis=0).reshape(2, 8, HC)

    slot = g % 2
    for z in range(2):
        here = (z * NP + s == g) & (g // 2 == s)

        @pl.when(here)
        def _():
            cp = pltpu.make_async_copy(AS.at[z], AR.at[slot], r1b.at[z])
            cp.start()
            cp.wait()

        @pl.when(jnp.logical_not(here))
        def _():
            rcopy(AS.at[z], AR.at[slot], 13 + z, z * NP + s, g // 2, r1c.at[slot]).start()
    for j in range(2):
        from_me = (2 * s + j == g) & (p == s)

        @pl.when(jnp.logical_not(from_me))
        def _():
            pltpu.make_async_copy(AR.at[j], AR.at[j], r1c.at[j]).wait()
    att = jnp.concatenate([AR[0], AR[1]], axis=1)
    NR[s] = jnp.broadcast_to(jnp.sum(att * att, axis=1, keepdims=True), (8, 128))
    to_tensor(15, lambda q: NR.at[s], NR.at[s])
    bulk(NR, NT - 1, rsem.at[15])
    tot = jnp.sum(NR[...], axis=0)[:, 0:1]
    post = att * lax.rsqrt(tot / D + EPS) * GPO[pl.ds(s, 1), :]
    out_ref[...] = (SPF[zh] + post).astype(BF16)

    bulk(COL, 2 * NZ - 1, ssem.at[0])
    bulk(X.at[0], NP - 1, ssem.at[1])
    bulk(X.at[0], NP, ssem.at[2])
    bulk(VS, NT - 1, ssem.at[3])
    bulk(VG, NT - 1, ssem.at[4])
    bulk(RS, NP - 1, ssem.at[5])
    zc.wait_send()
    bulk(SP, NT - 1, ssem.at[7])
    bulk(XS, NP - 1, ssem.at[8])
    bulk(PS, NP - 1, ssem.at[9])
    yc.wait_send()
    bulk(QR, NP - 1, ssem.at[11])
    bulk(OS, NT - 1, ssem.at[12])
    for z in range(2):
        here = (z * NP + s == g) & (g // 2 == s)

        @pl.when(jnp.logical_not(here))
        def _():
            pltpu.make_async_copy(AS.at[z], AS.at[z], ssem.at[13 + z]).wait()
    bulk(NR, NT - 1, ssem.at[15])


def local(mesh, resid, enc, enc_bias, ids, dec, dec_bias, segs, gin, gpo, qw, kw, vw, ow):
    NT = mesh.shape["tensor"]
    NP = mesh.shape["dp"] // 2
    assert NT == NP
    T, CH, NZ = 16 * NP, resid.shape[1], NT // 2
    HC = CH // 2
    V = pltpu.VMEM
    scratch = [
        V((2, NZ * CH, 256), BF16), V(dec.shape, BF16), V(qw.shape, BF16), V(kw.shape, BF16),
        V(vw.shape, BF16), V(ow.shape, BF16),
        V((2 * NZ, 8, CH), BF16), V((2, NP, 16, NZ * CH), BF16), V((8 * NP, 128), jnp.int32),
        V((NP, 1024, 256), BF16), V((NT, 8, 128), F32), V((NT, 8, 128), F32), V((NT, 8, 128), F32),
        V((NT, T, 256), BF16),
        V((NP, 16, CH), F32), V((NP, 16, CH), F32), V((16, CH), F32), V((16, CH), F32),
        V((2, 8, CH), F32), V((NT, 16, CH), BF16), V((NT, CH), F32), V((NT, CH), F32),
        V((NP, 16, HC), BF16), V((NP, 16, HC), BF16), V((NP, 16, 512), F32), V((NP, 16, 512), F32),
        V((16, 512), F32), V((16, 512), F32), V((NP, 16, 512), BF16),
        V((T, 128), F32), V((T, 128), F32), V((T, T), F32), V((T, 256), BF16),
        V((NT, 16, HC), F32), V((NT, 16, HC), F32), V((2, 8, HC), F32), V((2, 8, HC), F32),
        V((NT, 8, 128), F32),
        pltpu.SemaphoreType.DMA((2 * NZ + 5,)), pltpu.SemaphoreType.DMA((16,)),
        pltpu.SemaphoreType.DMA((16,)), pltpu.SemaphoreType.DMA((NP,)), pltpu.SemaphoreType.DMA((NP,)),
    ]
    vm = pl.BlockSpec(memory_space=V)
    hbm = pl.BlockSpec(memory_space=pl.ANY)
    return pl.pallas_call(
        lambda *refs: kernel(NP, NT, *refs),
        out_shape=jax.ShapeDtypeStruct((8, CH), BF16),
        in_specs=[vm, hbm, vm, vm, hbm, vm, vm, vm, vm, hbm, hbm, hbm, hbm],
        out_specs=vm,
        scratch_shapes=scratch,
        compiler_params=pltpu.CompilerParams(
            has_side_effects=True, vmem_limit_bytes=56 * 1024 * 1024),
    )(resid, enc, enc_bias[None], ids, dec, dec_bias[None], segs[None], gin[None], gpo[None],
      qw, kw, vw, ow)


def solution(mesh):
    return jax.shard_map(
        lambda *args: local(mesh, *args),
        mesh=mesh,
        in_specs=(
            P("dp", "tensor"),
            P(None, ("dp", "tensor")),
            P(("dp", "tensor")),
            P(),
            P("dp", "tensor"),
            P("tensor"),
            P(),
            P(),
            P(),
            P("dp", "tensor"),
            P("dp", "tensor"),
            P("dp", "tensor"),
            P("tensor", "dp"),
        ),
        out_specs=P("dp", "tensor"),
        check_vma=False,
    )
```

time: 1510 us -> 167 us (0.11)
  the two profiles are of different devices: /device:TPU:1 before, /device:TPU:25 now
where the time goes in v1:
time: 167 us; the launch traced here: 166 us
  Pallas kernels  153 us (92%)
  local copies, waits for them, and re-layouts  12.9 us (8%)
    pallas_call x1, Pallas kernels, local(): pl.pallas_call(lambda *refs: kernel(NP, NT, *refs), out_shape=jax.ShapeDt...  153 us
    unnamed x4, local copies, waits for them, and re-layouts  9 us

profile of v1, /device:TPU:25, one launch (start us, length us, event | category | flops | bytes accessed | tf_op | source)
XLA Modules:
  0.0 166.1 jit_solution(13457673521415163672)
XLA Ops:
  0.0 1.2 broadcast_in_dim.16.refs_5_
  1.2 1.3 broadcast_in_dim.18.refs_7_
  2.6 1.3 broadcast_in_dim.19.refs_8_
  3.9 1.6 copy.14.refs_3_
  5.5 1.6 copy.16.refs_12_
  7.1 4.5 %copy.15.refs_4_ = bf16[4096,288]{1,0:T(8,128)(2,1)} copy(bf16[4096,288]{0,1:T(8,128)(2,1)} %param.17) | data formatting | bytes 4718592 | tf_op args[4]
  11.6 153.2 %shard_map.127 = bf16[8,288]{1,0:T(8,128)(2,1)} custom-call(bf16[8,288]{1,0:T(8,128)(2,1)} %refs_0_.1, bf16[4608,256]{1,0:T(8,128)(2,1)} %refs_1_.1, f32[1,256]{1,0:T(1,128)} %bitcast.2, s32[256,64]{1,0:T(8,128)} %copy.14.refs_3_, bf16[4096,288]{1,0:T(8,128)(2,1)} %copy.15.refs_4_, f32[1,288]{1,0:T(1,128)} %broadcast_in_dim.16.refs_5_, s32[1,256]{1,0:T(1,128)} %bitcast.3, ...), custom_call_target="tpu_custom_call" | custom-call | tf_op jit(solution)/shard_map/pallas_call | solution.py:323
  164.8 1.3 copy.18

commit v2 on v1

v2 whole, which is shorter than its diff:
```python
import math

import jax
import jax.numpy as jnp
from jax import lax
from jax.experimental import pallas as pl
from jax.experimental.pallas import tpu as pltpu
from jax.sharding import PartitionSpec as P

QUERY_SCALE = 144.0 ** (-0.5)
SOFT_CAP = 50.0
EPS = 1e-06
MESH = pl.DeviceIdType.MESH
F32 = jnp.float32
BF16 = jnp.bfloat16


def dot_nt(a, b):
    return lax.dot_general(a, b, (((1,), (1,)), ((), ())), preferred_element_type=F32)


def kernel(
    NP, NT,
    resid, enc_hbm, enc_bias, ids_ref, dec_hbm, dec_bias, segs, gain_in, gain_post,
    q_hbm, k_hbm, v_hbm, o_hbm,
    out_ref,
    E, DEC, WA, WB,
    COL, X, IDT, IDP, B, VS, VR, VG, S,
    RS, RR, ZS, ZR, SPF, SP, GIN, GPO, YS, YR, QB, KV,
    CT, ST, MASK, HO, OSD, OSR, OSS, OR, NR,
    lsem, ssem, rsem, r1b, r1c, r7, r7b,
):
    T = 16 * NP
    R8 = 8 * NP
    NZ = NT // 2
    NH = NT // 2
    CH = resid.shape[1]
    D = NT * CH
    g = lax.axis_index("dp")
    s = lax.axis_index("tensor")
    zh = g // NP
    p = g % NP
    zl = s // 2
    c = s % 2
    sib = s + 1 - 2 * c

    def wrap(i, n):
        return jnp.where(i >= n, i - n, i)

    def rcopy(src, dst, k, dp, tensor, rs=None):
        return pltpu.make_async_remote_copy(
            src_ref=src, dst_ref=dst, send_sem=ssem.at[k],
            recv_sem=rsem.at[k] if rs is None else rs,
            device_id={"dp": dp, "tensor": tensor}, device_id_type=MESH)

    drains = []

    def bulk(ref, n, sem):
        d = ref.at[pl.ds(0, n)]
        pltpu.make_async_copy(d, d, sem).wait()

    def drain():
        for wait in drains:
            wait()

    def to_plane(k, src, dst, sent, rs=None):
        for j in range(1, NP):
            q = wrap(p + j, NP)
            rcopy(src(q), dst, k, zh * NP + q, s, rs).start()
        drains.append(lambda: bulk(sent, NP - 1, ssem.at[k]))

    def to_tensor(k, src, dst, sent):
        for j in range(1, NT):
            q = wrap(s + j, NT)
            rcopy(src(q), dst, k, g, q).start()
        drains.append(lambda: bulk(sent, NT - 1, ssem.at[k]))

    barrier = pltpu.get_barrier_semaphore()

    def greet(dp, tensor):
        pl.semaphore_signal(
            barrier, inc=1, device_id={"dp": dp, "tensor": tensor}, device_id_type=MESH)
    for j in range(1, NT):
        greet(g, wrap(s + j, NT))
    for j in range(NT):
        greet((1 - zh) * NP + p, j)
    for j in range(1, NP):
        greet(zh * NP + wrap(p + j, NP), s)

    loads = []
    for z in range(NZ):
        for h in range(2):
            row = pl.multiple_of((2 * z + (c if h == 0 else 1 - c)) * CH, 16)
            loads.append(pltpu.make_async_copy(
                enc_hbm.at[pl.ds(row, CH)], E.at[h, pl.ds(z * CH, CH)], lsem.at[len(loads)]))
    n_enc = len(loads)
    for a, b in (
        (dec_hbm, DEC), (q_hbm, WA.at[p, :, 0:256]), (k_hbm, WA.at[p, :, 256:384]),
        (v_hbm, WA.at[p, :, 384:512]), (o_hbm, WB.at[p]),
    ):
        loads.append(pltpu.make_async_copy(a, b, lsem.at[len(loads)]))
    for cp in loads:
        cp.start()
    me_z = zh * NZ + zl
    COL[me_z] = resid[...]

    IDT[...] = jnp.concatenate([ids_ref[:, :R8], ids_ref[:, R8:]], axis=0)
    IDP[...] = IDT[...].T
    gi, gp = gain_in[...][None], gain_post[...][None]
    for j in range(NT):
        GIN[j:j + 1, :] = gi[:, j * CH:(j + 1) * CH]
        GPO[j:j + 1, :] = gp[:, j * CH:(j + 1) * CH]

    def tok(r):
        return ((r // 8) % 2) * R8 + (r // 16) * 8 + r % 8
    segc = jnp.broadcast_to(segs[...].astype(F32)[None], (T, T)).T
    segc = jnp.concatenate(
        [segc[h * R8 + b * 8:h * R8 + b * 8 + 8] for b in range(NP) for h in range(2)], axis=0)
    tr = tok(lax.broadcasted_iota(jnp.int32, (T, T), 0))
    tc = tok(lax.broadcasted_iota(jnp.int32, (T, T), 1))
    same = segc == segc.T
    MASK[...] = jnp.where(same & (tc <= tr), 1.0, 0.0)
    pos = jnp.sum(jnp.where(same & (tc < tr), 1.0, 0.0), axis=1, keepdims=True)
    lane = lax.broadcasted_iota(jnp.int32, (1, 128), 1)
    inverse = jnp.exp((lane % 64).astype(F32) * (-2.0 * math.log(10000.0) / 128))
    ang = pos * inverse
    CT[...] = jnp.cos(ang)
    ST[...] = jnp.where(lane < 64, -1.0, 1.0) * jnp.sin(ang)

    pl.semaphore_wait(barrier, 2 * NT - 1 + NP - 1)
    for j in range(1, 2 * NZ):
        z = wrap(me_z + j, 2 * NZ)
        far = jnp.where(z >= NZ, 1, 0)
        rcopy(resid, COL.at[me_z], 0, far * NP + p, (z - far * NZ) * 2 + c).start()
    drains.append(lambda: bulk(COL, 2 * NZ - 1, ssem.at[0]))

    @pl.loop(0, NP)
    def _(b):
        lo = (IDP[pl.ds(pl.multiple_of(b * 8, 8), 8), :] & 255).astype(F32).T
        cols = lax.broadcasted_iota(jnp.int32, (128, 256), 1).astype(F32)
        for i in range(8):
            B[b, pl.ds(i * 128, 128), :] = jnp.where(lo[:, i:i + 1] == cols, 1.0, 0.0).astype(BF16)

    bulk(COL, 2 * NZ - 1, rsem.at[0])
    halves = []
    for h in range(2):
        halves.append(jnp.concatenate(
            [COL[h * NZ + z].astype(F32) for z in range(NZ)], axis=1))
    X[0, p] = jnp.concatenate(halves, axis=0).astype(BF16)
    to_plane(1, lambda q: X.at[0, p], X.at[0, p], X.at[0], r1b.at[p])
    rcopy(X.at[0, p], X.at[1, p], 2, g, sib, r1c.at[p]).start()
    drains.append(lambda: bulk(X.at[0], NP, ssem.at[2]))
    for j in range(1, NP):
        q = wrap(p + NP - j, NP)
        pltpu.make_async_copy(X.at[0, q], X.at[0, q], r1b.at[q]).wait()
        rcopy(X.at[0, q], X.at[1, q], 2, g, sib, r1c.at[q]).start()

    for cp in loads[n_enc + 1:]:
        cp.wait()
    to_plane(8, lambda q: WA.at[p], WA.at[p], WA)
    to_plane(9, lambda q: WB.at[p], WB.at[p], WB)

    for cp in loads[:n_enc]:
        cp.wait()
    pre = jnp.dot(X[0].reshape(T, NZ * CH), E[0], preferred_element_type=F32)
    for q in range(NP):
        pltpu.make_async_copy(X.at[1, q], X.at[1, q], r1c.at[q]).wait()
    pre = pre + jnp.dot(X[1].reshape(T, NZ * CH), E[1], preferred_element_type=F32)
    act = jnp.maximum(pre + enc_bias[...][None], 0.0).astype(BF16).astype(F32)

    act = act.reshape(NP, 2, 8, 256)
    a0 = act[:, 0].reshape(R8, 256)
    a1 = act[:, 1].reshape(R8, 256)
    rel = IDP[...] - (g * NT + s) * 256
    low = rel & 127
    left = lax.broadcasted_iota(jnp.int32, (R8, 128), 1) < 64

    def pick(h):
        return jnp.where(
            left,
            jnp.take_along_axis(a0[:, h * 128:(h + 1) * 128], low, axis=1),
            jnp.take_along_axis(a1[:, h * 128:(h + 1) * 128], low, axis=1))
    val = jnp.where(rel >= 128, pick(1), pick(0))
    val = jnp.where((rel >= 0) & (rel < 256), val, 0.0)
    VS[...] = val.reshape(NT, 8, 128)
    VR[s] = VS[s]
    to_tensor(3, lambda q: VS.at[q], VR.at[s], VS)
    bulk(VR, NT - 1, rsem.at[3])
    VG[s] = jnp.sum(VR[...], axis=0)
    to_tensor(4, lambda q: VG.at[s], VG.at[s], VG)
    bulk(VG, NT - 1, rsem.at[4])

    sub = lax.broadcasted_iota(jnp.int32, (8, 128), 0)
    lft = lax.broadcasted_iota(jnp.int32, (8, 128), 1) < 64
    @pl.loop(0, NP)
    def _(b):
        relb = IDP[pl.ds(pl.multiple_of(b * 8, 8), 8), :] - g * (NT * 256)
        vb = VG[b]
        hi = jnp.where(relb < 0, -1, relb >> 8)
        v0 = jnp.where(lft, vb, 0.0)
        v1 = vb - v0
        rows = []
        for h in range(NT):
            for vz in (v0, v1):
                d = jnp.where(hi == h, vz, 0.0)
                rows.append(jnp.concatenate([jnp.where(sub == i, d, 0.0) for i in range(8)], axis=1))
        lhs = jnp.concatenate(rows, axis=0).astype(BF16)
        sel = jnp.dot(lhs, B[b], preferred_element_type=F32).astype(BF16)
        S[:, pl.ds(pl.multiple_of(b * 16, 16), 16), :] = sel.reshape(NT, 16, 256)
    loads[n_enc].wait()
    rec = dot_nt(S[0], DEC[:, 0:256])
    for h in range(1, NT):
        rec = rec + dot_nt(S[h], DEC[:, h * 256:(h + 1) * 256])
    RS[...] = rec.reshape(NP, 16, CH)
    RR[p] = RS[p]
    to_plane(5, lambda q: RS.at[q], RR.at[p], RS)
    bulk(RR, NP - 1, rsem.at[5])
    ZS[...] = jnp.sum(RR[...], axis=0)
    zp = (1 - zh) * NP + p
    zc = rcopy(ZS, ZR, 6, zp, s)
    zc.start()
    drains.append(zc.wait_send)
    zc.wait_recv()
    spl = (ZS[...] + ZR[...] + dec_bias[...][None]).astype(BF16)
    SPF[...] = spl.astype(F32).reshape(2, 8, CH)
    SP[s] = spl

    rcopy(SP.at[s], SP.at[s], 10, g, sib, r7b.at[zl]).start()
    for j in range(1, NZ):
        rcopy(SP.at[s], SP.at[s], 7, g, 2 * wrap(zl + j, NZ) + c, r7.at[zl]).start()
    if NZ > 1:
        drains.append(lambda: bulk(SP, NZ - 1, ssem.at[7]))
    drains.append(lambda: bulk(SP, NZ, ssem.at[10]))
    for j in range(1, NZ):
        z = wrap(zl + NZ - j, NZ)
        there = SP.at[2 * z + c]
        pltpu.make_async_copy(there, there, r7.at[z]).wait()
        rcopy(there, there, 10, g, sib, r7b.at[z]).start()
    for z in range(NZ):
        pltpu.make_async_copy(SP.at[0], SP.at[0], r7b.at[z]).wait()

    ss = jnp.zeros((16, 1), F32)
    for j in range(NT):
        xj = SP[j].astype(F32)
        ss = ss + jnp.sum(xj * xj, axis=1, keepdims=True)
    rn = lax.rsqrt(ss / D + EPS)
    normed = []
    for j in range(NH):
        cj = zh * NH + j
        normed.append(SP[cj].astype(F32) * rn * GIN[pl.ds(cj, 1), :])
    normed = jnp.concatenate(normed, axis=1).astype(BF16)
    bulk(WA, NP - 1, rsem.at[8])
    YS[...] = jnp.dot(normed, WA[...].reshape(NH * CH, 512), preferred_element_type=F32)
    yc = rcopy(YS, YR, 11, zp, s)
    yc.start()
    drains.append(yc.wait_send)
    yc.wait_recv()
    y = YS[...] + YR[...]
    mine = pl.ds(pl.multiple_of(p * 16, 16), 16)
    cosine, sine = CT[mine, :], ST[mine, :]

    def rot(x):
        return x * cosine + pltpu.roll(x, 64, 1) * sine
    KV[p] = jnp.concatenate([rot(y[:, 256:384]), y[:, 384:512]], axis=1).astype(BF16)
    to_plane(12, lambda q: KV.at[p], KV.at[p], KV)
    QB[...] = jnp.concatenate(
        [rot(y[:, 0:128]) * QUERY_SCALE, rot(y[:, 128:256]) * QUERY_SCALE], axis=1).astype(BF16)
    bulk(KV, NP - 1, rsem.at[12])

    kk = KV[:, :, 0:128].reshape(T, 128)
    vv = KV[:, :, 128:256].reshape(T, 128)
    allowed = MASK[mine, :] > 0.0
    for h in range(2):
        sc = dot_nt(QB[:, h * 128:(h + 1) * 128], kk)
        w = jnp.where(allowed, jnp.exp(SOFT_CAP * jnp.tanh(sc / SOFT_CAP)), 0.0)
        tot = jnp.sum(w, axis=1, keepdims=True)
        mixed = jnp.dot(w.astype(BF16), vv, preferred_element_type=F32)
        HO[:, h * 128:(h + 1) * 128] = (mixed / tot).astype(BF16)
    bulk(WB, NP - 1, rsem.at[9])
    for j in range(NH):
        o = dot_nt(HO[...], WB[pl.ds(2 * j, 2)].reshape(CH, 256))
        OSD[0, j] = o[:8]
        OSD[1, j] = o[8:]

    oc = rcopy(OSD.at[1 - c], OSR, 13, g, sib)
    oc.start()
    drains.append(oc.wait_send)
    oc.wait_recv()
    OSS[...] = OSD[c] + OSR[...]
    own = (c == zh) & (s // NH == zh)
    for j in range(NH):
        here = (c == zh) & (zh * NH + j == s)

        @pl.when(here)
        def _():
            OR[zl] = OSS[j]

        @pl.when(jnp.logical_not(here))
        def _():
            rcopy(OSS.at[j], OR.at[zl], 14, c * NP + p, zh * NH + j).start()

    def bulk_own(ref, sem):
        @pl.when(own)
        def _():
            if NZ > 1:
                bulk(ref, NZ - 1, sem)

        @pl.when(jnp.logical_not(own))
        def _():
            bulk(ref, NZ, sem)
    drains.append(lambda: bulk_own(OSS, ssem.at[14]))
    bulk_own(OR, rsem.at[14])
    att = jnp.sum(OR[...], axis=0)
    NR[s] = jnp.broadcast_to(jnp.sum(att * att, axis=1, keepdims=True), (8, 128))
    to_tensor(15, lambda q: NR.at[s], NR.at[s], NR)
    bulk(NR, NT - 1, rsem.at[15])
    tot = jnp.sum(NR[...], axis=0)[:, 0:1]
    post = att * lax.rsqrt(tot / D + EPS) * GPO[pl.ds(s, 1), :]
    out_ref[...] = (SPF[zh] + post).astype(BF16)
    drain()


def local(mesh, resid, enc, enc_bias, ids, dec, dec_bias, segs, gin, gpo, qw, kw, vw, ow):
    NT = mesh.shape["tensor"]
    NP = mesh.shape["dp"] // 2
    assert NT == NP
    T, CH, NZ = 16 * NP, resid.shape[1], NT // 2
    HC = CH // 2
    V = pltpu.VMEM
    scratch = [
        V((2, NZ * CH, 256), BF16), V(dec.shape[::-1], BF16), V((NP, HC, 512), BF16),
        V((NP, HC, 256), BF16),
        V((2 * NZ, 8, CH), BF16), V((2, NP, 16, NZ * CH), BF16), V((128, 8 * NP), jnp.int32),
        V((8 * NP, 128), jnp.int32), V((NP, 1024, 256), BF16),
        V((NT, 8, 128), F32), V((NT, 8, 128), F32), V((NT, 8, 128), F32), V((NT, T, 256), BF16),
        V((NP, 16, CH), F32), V((NP, 16, CH), F32), V((16, CH), F32), V((16, CH), F32),
        V((2, 8, CH), F32), V((NT, 16, CH), BF16), V((NT, CH), F32), V((NT, CH), F32),
        V((16, 512), F32), V((16, 512), F32), V((16, 256), BF16), V((NP, 16, 256), BF16),
        V((T, 128), F32), V((T, 128), F32), V((T, T), F32), V((16, 256), BF16),
        V((2, NZ, 8, CH), F32), V((NZ, 8, CH), F32), V((NZ, 8, CH), F32), V((NZ, 8, CH), F32),
        V((NT, 8, 128), F32),
        pltpu.SemaphoreType.DMA((2 * NZ + 5,)), pltpu.SemaphoreType.DMA((16,)),
        pltpu.SemaphoreType.DMA((16,)), pltpu.SemaphoreType.DMA((NP,)), pltpu.SemaphoreType.DMA((NP,)),
        pltpu.SemaphoreType.DMA((NZ,)), pltpu.SemaphoreType.DMA((NZ,)),
    ]
    vm = pl.BlockSpec(memory_space=V)
    hbm = pl.BlockSpec(memory_space=pl.ANY)
    return pl.pallas_call(
        lambda *refs: kernel(NP, NT, *refs),
        out_shape=jax.ShapeDtypeStruct((8, CH), BF16),
        in_specs=[vm, hbm, vm, vm, hbm, vm, vm, vm, vm, hbm, hbm, hbm, hbm],
        out_specs=vm,
        scratch_shapes=scratch,
        compiler_params=pltpu.CompilerParams(
            collective_id=0, has_side_effects=True, vmem_limit_bytes=56 * 1024 * 1024),
    )(resid, enc, enc_bias, ids.T, dec.T, dec_bias, segs, gin, gpo, qw, kw, vw, ow.T)


def solution(mesh):
    return jax.shard_map(
        lambda *args: local(mesh, *args),
        mesh=mesh,
        in_specs=(
            P("dp", "tensor"),
            P(None, ("dp", "tensor")),
            P(("dp", "tensor")),
            P(),
            P("dp", "tensor"),
            P("tensor"),
            P(),
            P(),
            P(),
            P("dp", "tensor"),
            P("dp", "tensor"),
            P("dp", "tensor"),
            P("tensor", "dp"),
        ),
        out_specs=P("dp", "tensor"),
        check_vma=False,
    )
```

time: 167 us -> 140 us (0.84)
  the two profiles are of different devices: /device:TPU:25 before, /device:TPU:1 now
where the time goes in v2:
time: 140 us
  Pallas kernels  139 us (99%)
    pallas_call x1, Pallas kernels, local(): pl.pallas_call(lambda *refs: kernel(NP, NT, *refs), out_shape=jax.ShapeDt...  139 us

profile of v2, /device:TPU:1, one launch (start us, length us, event | category | flops | bytes accessed | tf_op | source)
XLA Modules:
  0.0 140.0 jit_solution(1044486597187301858)
XLA Ops:
  0.0 138.7 %shard_map.127 = bf16[8,288]{1,0:T(8,128)(2,1)} custom-call(bf16[8,288]{1,0:T(8,128)(2,1)} %refs_0_.1, bf16[4608,256]{1,0:T(8,128)(2,1)} %refs_1_.1, f32[256]{0:T(256)} %refs_2_.1, s32[64,256]{1,0:T(8,128)} %bitcast.5, bf16[288,4096]{1,0:T(8,128)(2,1)} %bitcast.3, f32[288]{0:T(512)} %refs_5_.1, s32[256]{0:T(256)} %refs_6_.1, f32[4608]{0:T(1024)} %refs_7_.1, ...), custom_call_target="tpu_custom_call" | custom-call | tf_op jit(solution)/shard_map/pallas_call | solution.py:348
  138.8 1.3 copy.15

commit v3 on v2

--- a/solution.py
+++ b/solution.py
@@ -20,15 +20,15 @@
 
 
 def kernel(
-    NP, NT,
+    NP, NT, NX, NY,
     resid, enc_hbm, enc_bias, ids_ref, dec_hbm, dec_bias, segs, gain_in, gain_post,
     q_hbm, k_hbm, v_hbm, o_hbm,
     out_ref,
-    E, DEC, WA, WB,
+    E, DEC, WQ, WK, WB,
     COL, X, IDT, IDP, B, VS, VR, VG, S,
-    RS, RR, ZS, ZR, SPF, SP, GIN, GPO, YS, YR, QB, KV,
-    CT, ST, MASK, HO, OSD, OSR, OSS, OR, NR,
-    lsem, ssem, rsem, r1b, r1c, r7, r7b,
+    RS, RR, ZS, ZR, SPF, SP, GIN, GPO, YKS, YKR, YQS, YQR, QB, KV,
+    SEGC, HO, OSD, OSR, OSS, OR, NR,
+    lsem, ssem, rsem, r2x, r2y, r7, r7b,
 ):
     T = 16 * NP
     R8 = 8 * NP
@@ -42,6 +42,8 @@
     p = g % NP
     zl = s // 2
     c = s % 2
+    x = p % NX
+    y = p // NX
     sib = s + 1 - 2 * c
 
     def wrap(i, n):
@@ -59,6 +61,9 @@
         d = ref.at[pl.ds(0, n)]
         pltpu.make_async_copy(d, d, sem).wait()
 
+    def land(ref, sem):
+        pltpu.make_async_copy(ref, ref, sem).wait()
+
     def drain():
         for wait in drains:
             wait()
@@ -68,6 +73,16 @@
             q = wrap(p + j, NP)
             rcopy(src(q), dst, k, zh * NP + q, s, rs).start()
         drains.append(lambda: bulk(sent, NP - 1, ssem.at[k]))
+
+    def to_x(k, src, dst, many, rs=None):
+        for j in range(1, NX):
+            rcopy(src, dst, k, zh * NP + y * NX + wrap(x + j, NX), s, rs).start()
+        drains.append(lambda: land(many, ssem.at[k]))
+
+    def to_y(k, src, dst, many, rs=None):
+        for j in range(1, NY):
+            rcopy(src, dst, k, zh * NP + wrap(y + j, NY) * NX + x, s, rs).start()
+        drains.append(lambda: land(many, ssem.at[k]))
 
     def to_tensor(k, src, dst, sent):
         for j in range(1, NT):
@@ -95,8 +110,8 @@
                 enc_hbm.at[pl.ds(row, CH)], E.at[h, pl.ds(z * CH, CH)], lsem.at[len(loads)]))
     n_enc = len(loads)
     for a, b in (
-        (dec_hbm, DEC), (q_hbm, WA.at[p, :, 0:256]), (k_hbm, WA.at[p, :, 256:384]),
-        (v_hbm, WA.at[p, :, 384:512]), (o_hbm, WB.at[p]),
+        (dec_hbm, DEC), (q_hbm, WQ.at[y, x]), (k_hbm, WK.at[y, x, :, 0:128]),
+        (v_hbm, WK.at[y, x, :, 128:256]), (o_hbm, WB.at[y, x]),
     ):
         loads.append(pltpu.make_async_copy(a, b, lsem.at[len(loads)]))
     for cp in loads:
@@ -111,21 +126,22 @@
         GIN[j:j + 1, :] = gi[:, j * CH:(j + 1) * CH]
         GPO[j:j + 1, :] = gp[:, j * CH:(j + 1) * CH]
 
-    def tok(r):
-        return ((r // 8) % 2) * R8 + (r // 16) * 8 + r % 8
-    segc = jnp.broadcast_to(segs[...].astype(F32)[None], (T, T)).T
-    segc = jnp.concatenate(
+    segc = jnp.broadcast_to(segs[...].astype(F32)[None], (128, T)).T
+    SEGC[...] = jnp.concatenate(
         [segc[h * R8 + b * 8:h * R8 + b * 8 + 8] for b in range(NP) for h in range(2)], axis=0)
-    tr = tok(lax.broadcasted_iota(jnp.int32, (T, T), 0))
-    tc = tok(lax.broadcasted_iota(jnp.int32, (T, T), 1))
-    same = segc == segc.T
-    MASK[...] = jnp.where(same & (tc <= tr), 1.0, 0.0)
+    mine = pl.ds(pl.multiple_of(p * 16, 16), 16)
+    same = SEGC[mine, :][:, 0:1] == SEGC[...].T[0:1, :]
+    row = lax.broadcasted_iota(jnp.int32, (16, 1), 0)
+    col = lax.broadcasted_iota(jnp.int32, (1, T), 1)
+    tr = (row >> 3) * R8 + p * 8 + (row & 7)
+    tc = ((col >> 3) & 1) * R8 + (col >> 4) * 8 + (col & 7)
+    allowed = same & (tc <= tr)
     pos = jnp.sum(jnp.where(same & (tc < tr), 1.0, 0.0), axis=1, keepdims=True)
     lane = lax.broadcasted_iota(jnp.int32, (1, 128), 1)
-    inverse = jnp.exp((lane % 64).astype(F32) * (-2.0 * math.log(10000.0) / 128))
+    inverse = jnp.exp((lane & 63).astype(F32) * (-2.0 * math.log(10000.0) / 128))
     ang = pos * inverse
-    CT[...] = jnp.cos(ang)
-    ST[...] = jnp.where(lane < 64, -1.0, 1.0) * jnp.sin(ang)
+    cosine = jnp.cos(ang)
+    sine = jnp.where(lane < 64, -1.0, 1.0) * jnp.sin(ang)
 
     pl.semaphore_wait(barrier, 2 * NT - 1 + NP - 1)
     for j in range(1, 2 * NZ):
@@ -146,26 +162,61 @@
     for h in range(2):
         halves.append(jnp.concatenate(
             [COL[h * NZ + z].astype(F32) for z in range(NZ)], axis=1))
-    X[0, p] = jnp.concatenate(halves, axis=0).astype(BF16)
-    to_plane(1, lambda q: X.at[0, p], X.at[0, p], X.at[0], r1b.at[p])
-    rcopy(X.at[0, p], X.at[1, p], 2, g, sib, r1c.at[p]).start()
-    drains.append(lambda: bulk(X.at[0], NP, ssem.at[2]))
-    for j in range(1, NP):
-        q = wrap(p + NP - j, NP)
-        pltpu.make_async_copy(X.at[0, q], X.at[0, q], r1b.at[q]).wait()
-        rcopy(X.at[0, q], X.at[1, q], 2, g, sib, r1c.at[q]).start()
+    X[0, y, x] = jnp.concatenate(halves, axis=0).astype(BF16)
+    F2 = NZ * CH
+    A, Bh = pl.ds(0, F2 // 2), pl.ds(F2 // 2, F2 // 2)
+
+    def on(*where):
+        rcopy(X.at[(0,) + where], X.at[(1,) + where], 2, g, sib, rsem.at[2]).start()
+    own_a, own_b = X.at[0, y, x, :, A], X.at[0, y, x, :, Bh]
+    row_a, col_b = X.at[0, y, :, :, A], X.at[0, :, x, :, Bh]
+    own_as, own_bs = X.at[0, y, pl.ds(0, NX - 1), :, A], X.at[0, pl.ds(0, NY - 1), x, :, Bh]
+    row_as, col_bs = X.at[0, pl.ds(0, NY - 1), :, :, A], X.at[0, :, pl.ds(0, NX - 1), :, Bh]
+    to_x(1, own_a, own_a, own_as)
+    to_y(17, own_b, own_b, own_bs)
+    land(own_as, rsem.at[1])
+    to_y(18, row_a, row_a, row_as, r2y.at[y])
+    land(own_bs, rsem.at[17])
+    to_x(19, col_b, col_b, col_bs, r2x.at[x])
+    on(y, slice(None), slice(None), A)
+    on(slice(None), x, slice(None), Bh)
 
     for cp in loads[n_enc + 1:]:
         cp.wait()
-    to_plane(8, lambda q: WA.at[p], WA.at[p], WA)
-    to_plane(9, lambda q: WB.at[p], WB.at[p], WB)
+    lo, hi = pl.ds(0, 80), pl.ds(80, 64)
+    nx, ny = pl.ds(0, NX - 1), pl.ds(0, NY - 1)
+    own_q, own_k, own_ba, own_bb = WQ.at[y, x], WK.at[y, x], WB.at[y, x, lo], WB.at[y, x, hi]
+    own_qs, own_ks, own_bas, own_bbs = WQ.at[y, nx], WK.at[ny, x], WB.at[y, nx, lo], WB.at[ny, x, hi]
+    row_q, col_k, row_b, col_bb = WQ.at[y], WK.at[:, x], WB.at[y, :, lo], WB.at[:, x, hi]
+    row_qs, col_ks, row_bs, col_bbs = WQ.at[ny], WK.at[:, nx], WB.at[ny, :, lo], WB.at[:, nx, hi]
+    to_x(8, own_q, own_q, own_qs)
+    to_y(9, own_k, own_k, own_ks)
+    to_x(16, own_ba, own_ba, own_bas)
+    to_y(20, own_bb, own_bb, own_bbs)
+    for j in range(1, max(NX, NY)):
+        if j < NY:
+            yy = wrap(y + NY - j, NY)
+            land(row_a, r2y.at[yy])
+            on(yy, slice(None), slice(None), A)
+        if j < NX:
+            xx = wrap(x + NX - j, NX)
+            land(col_b, r2x.at[xx])
+            on(slice(None), xx, slice(None), Bh)
+    drains.append(lambda: land(X.at[0], ssem.at[2]))
+    land(own_qs, rsem.at[8])
+    to_y(21, row_q, row_q, row_qs)
+    land(own_ks, rsem.at[9])
+    to_x(22, col_k, col_k, col_ks)
+    land(own_bas, rsem.at[16])
+    to_y(23, row_b, row_b, row_bs)
+    land(own_bbs, rsem.at[20])
+    to_x(24, col_bb, col_bb, col_bbs)
 
     for cp in loads[:n_enc]:
         cp.wait()
-    pre = jnp.dot(X[0].reshape(T, NZ * CH), E[0], preferred_element_type=F32)
-    for q in range(NP):
-        pltpu.make_async_copy(X.at[1, q], X.at[1, q], r1c.at[q]).wait()
-    pre = pre + jnp.dot(X[1].reshape(T, NZ * CH), E[1], preferred_element_type=F32)
+    pre = jnp.dot(X[0].reshape(T, F2), E[0], preferred_element_type=F32)
+    land(X.at[1], rsem.at[2])
+    pre = pre + jnp.dot(X[1].reshape(T, F2), E[1], preferred_element_type=F32)
     act = jnp.maximum(pre + enc_bias[...][None], 0.0).astype(BF16).astype(F32)
 
     act = act.reshape(NP, 2, 8, 256)
@@ -182,11 +233,11 @@
             jnp.take_along_axis(a1[:, h * 128:(h + 1) * 128], low, axis=1))
     val = jnp.where(rel >= 128, pick(1), pick(0))
     val = jnp.where((rel >= 0) & (rel < 256), val, 0.0)
-    VS[...] = val.reshape(NT, 8, 128)
+    VS[...] = val.reshape(NT, 8, 128).astype(BF16)
     VR[s] = VS[s]
     to_tensor(3, lambda q: VS.at[q], VR.at[s], VS)
     bulk(VR, NT - 1, rsem.at[3])
-    VG[s] = jnp.sum(VR[...], axis=0)
+    VG[s] = jnp.sum(VR[...].astype(F32), axis=0).astype(BF16)
     to_tensor(4, lambda q: VG.at[s], VG.at[s], VG)
     bulk(VG, NT - 1, rsem.at[4])
 
@@ -195,7 +246,7 @@
     @pl.loop(0, NP)
     def _(b):
         relb = IDP[pl.ds(pl.multiple_of(b * 8, 8), 8), :] - g * (NT * 256)
-        vb = VG[b]
+        vb = VG[b].astype(F32)
         hi = jnp.where(relb < 0, -1, relb >> 8)
         v0 = jnp.where(lft, vb, 0.0)
         v1 = vb - v0
@@ -249,36 +300,42 @@
         cj = zh * NH + j
         normed.append(SP[cj].astype(F32) * rn * GIN[pl.ds(cj, 1), :])
     normed = jnp.concatenate(normed, axis=1).astype(BF16)
-    bulk(WA, NP - 1, rsem.at[8])
-    YS[...] = jnp.dot(normed, WA[...].reshape(NH * CH, 512), preferred_element_type=F32)
-    yc = rcopy(YS, YR, 11, zp, s)
-    yc.start()
-    drains.append(yc.wait_send)
-    yc.wait_recv()
-    y = YS[...] + YR[...]
-    mine = pl.ds(pl.multiple_of(p * 16, 16), 16)
-    cosine, sine = CT[mine, :], ST[mine, :]
-
-    def rot(x):
-        return x * cosine + pltpu.roll(x, 64, 1) * sine
-    KV[p] = jnp.concatenate([rot(y[:, 256:384]), y[:, 384:512]], axis=1).astype(BF16)
+    land(col_ks, rsem.at[22])
+    YKS[...] = jnp.dot(normed, WK[...].reshape(NH * CH, 256), preferred_element_type=F32)
+    kc = rcopy(YKS, YKR, 11, zp, s)
+    kc.start()
+    drains.append(kc.wait_send)
+    land(row_qs, rsem.at[21])
+    YQS[...] = jnp.dot(normed, WQ[...].reshape(NH * CH, 256), preferred_element_type=F32)
+    qc = rcopy(YQS, YQR, 25, zp, s)
+    qc.start()
+    drains.append(qc.wait_send)
+
+    def rot(v):
+        return v * cosine + pltpu.roll(v, 64, 1) * sine
+    kc.wait_recv()
+    kv = YKS[...] + YKR[...]
+    KV[p] = jnp.concatenate([rot(kv[:, 0:128]), kv[:, 128:256]], axis=1).astype(BF16)
     to_plane(12, lambda q: KV.at[p], KV.at[p], KV)
+    qc.wait_recv()
+    qs = YQS[...] + YQR[...]
     QB[...] = jnp.concatenate(
-        [rot(y[:, 0:128]) * QUERY_SCALE, rot(y[:, 128:256]) * QUERY_SCALE], axis=1).astype(BF16)
+        [rot(qs[:, 0:128]) * QUERY_SCALE, rot(qs[:, 128:256]) * QUERY_SCALE], axis=1).astype(BF16)
     bulk(KV, NP - 1, rsem.at[12])
 
     kk = KV[:, :, 0:128].reshape(T, 128)
     vv = KV[:, :, 128:256].reshape(T, 128)
-    allowed = MASK[mine, :] > 0.0
     for h in range(2):
         sc = dot_nt(QB[:, h * 128:(h + 1) * 128], kk)
         w = jnp.where(allowed, jnp.exp(SOFT_CAP * jnp.tanh(sc / SOFT_CAP)), 0.0)
         tot = jnp.sum(w, axis=1, keepdims=True)
         mixed = jnp.dot(w.astype(BF16), vv, preferred_element_type=F32)
         HO[:, h * 128:(h + 1) * 128] = (mixed / tot).astype(BF16)
-    bulk(WB, NP - 1, rsem.at[9])
+    land(row_bs, rsem.at[23])
+    land(col_bbs, rsem.at[24])
+    wb = WB[...].reshape(NH * CH, 256)
     for j in range(NH):
-        o = dot_nt(HO[...], WB[pl.ds(2 * j, 2)].reshape(CH, 256))
+        o = dot_nt(HO[...], wb[j * CH:(j + 1) * CH])
         OSD[0, j] = o[:8]
         OSD[1, j] = o[8:]
 
@@ -311,10 +368,11 @@
     drains.append(lambda: bulk_own(OSS, ssem.at[14]))
     bulk_own(OR, rsem.at[14])
     att = jnp.sum(OR[...], axis=0)
-    NR[s] = jnp.broadcast_to(jnp.sum(att * att, axis=1, keepdims=True), (8, 128))
+    diag = lax.broadcasted_iota(jnp.int32, (8, 128), 0) == lax.broadcasted_iota(jnp.int32, (8, 128), 1)
+    NR[s] = jnp.sum(jnp.where(diag, jnp.sum(att * att, axis=1, keepdims=True), 0.0), axis=0, keepdims=True)
     to_tensor(15, lambda q: NR.at[s], NR.at[s], NR)
     bulk(NR, NT - 1, rsem.at[15])
-    tot = jnp.sum(NR[...], axis=0)[:, 0:1]
+    tot = jnp.sum(jnp.where(diag, jnp.sum(NR[...], axis=0), 0.0), axis=1, keepdims=True)
     post = att * lax.rsqrt(tot / D + EPS) * GPO[pl.ds(s, 1), :]
     out_ref[...] = (SPF[zh] + post).astype(BF16)
     drain()
@@ -326,27 +384,29 @@
     assert NT == NP
     T, CH, NZ = 16 * NP, resid.shape[1], NT // 2
     HC = CH // 2
+    NX = 1 << (NP.bit_length() // 2)
+    NY = NP // NX
     V = pltpu.VMEM
     scratch = [
-        V((2, NZ * CH, 256), BF16), V(dec.shape[::-1], BF16), V((NP, HC, 512), BF16),
-        V((NP, HC, 256), BF16),
-        V((2 * NZ, 8, CH), BF16), V((2, NP, 16, NZ * CH), BF16), V((128, 8 * NP), jnp.int32),
+        V((2, NZ * CH, 256), BF16), V(dec.shape[::-1], BF16), V((NY, NX, HC, 256), BF16),
+        V((NY, NX, HC, 256), BF16), V((NY, NX, HC, 256), BF16),
+        V((2 * NZ, 8, CH), BF16), V((2, NY, NX, 16, NZ * CH), BF16), V((128, 8 * NP), jnp.int32),
         V((8 * NP, 128), jnp.int32), V((NP, 1024, 256), BF16),
-        V((NT, 8, 128), F32), V((NT, 8, 128), F32), V((NT, 8, 128), F32), V((NT, T, 256), BF16),
+        V((NT, 8, 128), BF16), V((NT, 8, 128), BF16), V((NT, 8, 128), BF16), V((NT, T, 256), BF16),
         V((NP, 16, CH), F32), V((NP, 16, CH), F32), V((16, CH), F32), V((16, CH), F32),
         V((2, 8, CH), F32), V((NT, 16, CH), BF16), V((NT, CH), F32), V((NT, CH), F32),
-        V((16, 512), F32), V((16, 512), F32), V((16, 256), BF16), V((NP, 16, 256), BF16),
-        V((T, 128), F32), V((T, 128), F32), V((T, T), F32), V((16, 256), BF16),
+        V((16, 256), F32), V((16, 256), F32), V((16, 256), F32), V((16, 256), F32), V((16, 256), BF16), V((NP, 16, 256), BF16),
+        V((T, 128), F32), V((16, 256), BF16),
         V((2, NZ, 8, CH), F32), V((NZ, 8, CH), F32), V((NZ, 8, CH), F32), V((NZ, 8, CH), F32),
-        V((NT, 8, 128), F32),
-        pltpu.SemaphoreType.DMA((2 * NZ + 5,)), pltpu.SemaphoreType.DMA((16,)),
-        pltpu.SemaphoreType.DMA((16,)), pltpu.SemaphoreType.DMA((NP,)), pltpu.SemaphoreType.DMA((NP,)),
+        V((NT, 1, 128), F32),
+        pltpu.SemaphoreType.DMA((2 * NZ + 5,)), pltpu.SemaphoreType.DMA((26,)),
+        pltpu.SemaphoreType.DMA((26,)), pltpu.SemaphoreType.DMA((NX,)), pltpu.SemaphoreType.DMA((NY,)),
         pltpu.SemaphoreType.DMA((NZ,)), pltpu.SemaphoreType.DMA((NZ,)),
     ]
     vm = pl.BlockSpec(memory_space=V)
     hbm = pl.BlockSpec(memory_space=pl.ANY)
     return pl.pallas_call(
-        lambda *refs: kernel(NP, NT, *refs),
+        lambda *refs: kernel(NP, NT, NX, NY, *refs),
         out_shape=jax.ShapeDtypeStruct((8, CH), BF16),
         in_specs=[vm, hbm, vm, vm, hbm, vm, vm, vm, vm, hbm, hbm, hbm, hbm],
         out_specs=vm,

time: 140 us -> 124 us (0.89)
  Pallas kernels: 139 us -> 122 us
    pallas_call x1, Pallas kernels: 139 us -> 122 us  [local(): pl.pallas_call(lambda *refs: kernel(NP, NT, NX, NY, *refs), out_shape=jax...]
where the time goes in v3:
time: 124 us
  Pallas kernels  122 us (98%)
  local copies, waits for them, and re-layouts  1.29 us (1%)
    pallas_call x1, Pallas kernels, local(): pl.pallas_call(lambda *refs: kernel(NP, NT, NX, NY, *refs), out_shape=jax...  122 us

profile of v3, /device:TPU:1, one launch (start us, length us, event | category | flops | bytes accessed | tf_op | source)
XLA Modules:
  0.0 123.7 jit_solution(5712521182224593343)
XLA Ops:
  0.0 122.4 %shard_map.127 = bf16[8,288]{1,0:T(8,128)(2,1)} custom-call(bf16[8,288]{1,0:T(8,128)(2,1)} %refs_0_.1, bf16[4608,256]{1,0:T(8,128)(2,1)} %refs_1_.1, f32[256]{0:T(256)} %refs_2_.1, s32[64,256]{1,0:T(8,128)} %bitcast.5, bf16[288,4096]{1,0:T(8,128)(2,1)} %bitcast.3, f32[288]{0:T(512)} %refs_5_.1, s32[256]{0:T(256)} %refs_6_.1, f32[4608]{0:T(1024)} %refs_7_.1, ...), custom_call_target="tpu_custom_call" | custom-call | tf_op jit(solution)/shard_map/pallas_call | solution.py:408
  122.4 1.3 %copy.15 = bf16[8,288]{1,0:T(8,128)(2,1)} copy(bf16[8,288]{1,0:T(8,128)(2,1)} %shard_map.127) | data formatting | bytes 9216

commit v4 on v3

--- a/solution.py
+++ b/solution.py
@@ -189,10 +189,6 @@
     own_qs, own_ks, own_bas, own_bbs = WQ.at[y, nx], WK.at[ny, x], WB.at[y, nx, lo], WB.at[ny, x, hi]
     row_q, col_k, row_b, col_bb = WQ.at[y], WK.at[:, x], WB.at[y, :, lo], WB.at[:, x, hi]
     row_qs, col_ks, row_bs, col_bbs = WQ.at[ny], WK.at[:, nx], WB.at[ny, :, lo], WB.at[:, nx, hi]
-    to_x(8, own_q, own_q, own_qs)
-    to_y(9, own_k, own_k, own_ks)
-    to_x(16, own_ba, own_ba, own_bas)
-    to_y(20, own_bb, own_bb, own_bbs)
     for j in range(1, max(NX, NY)):
         if j < NY:
             yy = wrap(y + NY - j, NY)
@@ -203,14 +199,10 @@
             land(col_b, r2x.at[xx])
             on(slice(None), xx, slice(None), Bh)
     drains.append(lambda: land(X.at[0], ssem.at[2]))
-    land(own_qs, rsem.at[8])
-    to_y(21, row_q, row_q, row_qs)
-    land(own_ks, rsem.at[9])
-    to_x(22, col_k, col_k, col_ks)
-    land(own_bas, rsem.at[16])
-    to_y(23, row_b, row_b, row_bs)
-    land(own_bbs, rsem.at[20])
-    to_x(24, col_bb, col_bb, col_bbs)
+    to_x(8, own_q, own_q, own_qs)
+    to_y(9, own_k, own_k, own_ks)
+    to_x(16, own_ba, own_ba, own_bas)
+    to_y(20, own_bb, own_bb, own_bbs)
 
     for cp in loads[:n_enc]:
         cp.wait()
@@ -234,16 +226,46 @@
     val = jnp.where(rel >= 128, pick(1), pick(0))
     val = jnp.where((rel >= 0) & (rel < 256), val, 0.0)
     VS[...] = val.reshape(NT, 8, 128).astype(BF16)
-    VR[s] = VS[s]
-    to_tensor(3, lambda q: VS.at[q], VR.at[s], VS)
-    bulk(VR, NT - 1, rsem.at[3])
-    VG[s] = jnp.sum(VR[...].astype(F32), axis=0).astype(BF16)
-    to_tensor(4, lambda q: VG.at[s], VG.at[s], VG)
-    bulk(VG, NT - 1, rsem.at[4])
+    first, NB = NT // 2 - 2, NT // 4
+    middle = (s >= first) & (s < first + 4)
+    part = pl.ds(jnp.where(middle, s - first, 0) * NB, NB)
+    for k in range(4):
+        @pl.when(s != first + k)
+        def _():
+            rcopy(VS.at[pl.ds(k * NB, NB)], VR.at[s], 3, g, first + k).start()
+    land(own_qs, rsem.at[8])
+    to_y(21, row_q, row_q, row_qs)
+    land(own_ks, rsem.at[9])
+    to_x(22, col_k, col_k, col_ks)
+
+    @pl.when(middle)
+    def _():
+        VR[s] = VS[part]
+        bulk(VR, NT - 1, rsem.at[3])
+        VG[part] = jnp.sum(VR[...].astype(F32), axis=0).astype(BF16)
+        for j in range(1, NT):
+            rcopy(VG.at[part], VG.at[part], 4, g, wrap(s + j, NT)).start()
+
+    def slots(sem, ref):
+        @pl.when(middle)
+        def _():
+            bulk(ref, 3 * NB, sem)
+
+        @pl.when(jnp.logical_not(middle))
+        def _():
+            bulk(ref, 4 * NB, sem)
+
+    def spread():
+        @pl.when(middle)
+        def _():
+            bulk(VR, NT - 1, ssem.at[4])
+    drains.append(lambda: slots(ssem.at[3], VS))
+    drains.append(spread)
+    slots(rsem.at[4], VG)
 
     sub = lax.broadcasted_iota(jnp.int32, (8, 128), 0)
     lft = lax.broadcasted_iota(jnp.int32, (8, 128), 1) < 64
-    @pl.loop(0, NP)
+    @pl.loop(0, NP, unroll=4)
     def _(b):
         relb = IDP[pl.ds(pl.multiple_of(b * 8, 8), 8), :] - g * (NT * 256)
         vb = VG[b].astype(F32)
@@ -266,6 +288,10 @@
     RR[p] = RS[p]
     to_plane(5, lambda q: RS.at[q], RR.at[p], RS)
     bulk(RR, NP - 1, rsem.at[5])
+    land(own_bas, rsem.at[16])
+    to_y(23, row_b, row_b, row_bs)
+    land(own_bbs, rsem.at[20])
+    to_x(24, col_bb, col_bb, col_bbs)
     ZS[...] = jnp.sum(RR[...], axis=0)
     zp = (1 - zh) * NP + p
     zc = rcopy(ZS, ZR, 6, zp, s)
@@ -392,7 +418,7 @@
         V((NY, NX, HC, 256), BF16), V((NY, NX, HC, 256), BF16),
         V((2 * NZ, 8, CH), BF16), V((2, NY, NX, 16, NZ * CH), BF16), V((128, 8 * NP), jnp.int32),
         V((8 * NP, 128), jnp.int32), V((NP, 1024, 256), BF16),
-        V((NT, 8, 128), BF16), V((NT, 8, 128), BF16), V((NT, 8, 128), BF16), V((NT, T, 256), BF16),
+        V((NT, 8, 128), BF16), V((NT, NT // 4, 8, 128), BF16), V((NT, 8, 128), BF16), V((NT, T, 256), BF16),
         V((NP, 16, CH), F32), V((NP, 16, CH), F32), V((16, CH), F32), V((16, CH), F32),
         V((2, 8, CH), F32), V((NT, 16, CH), BF16), V((NT, CH), F32), V((NT, CH), F32),
         V((16, 256), F32), V((16, 256), F32), V((16, 256), F32), V((16, 256), F32), V((16, 256), BF16), V((NP, 16, 256), BF16),

time: 124 us -> 112 us (0.903)
  Pallas kernels: 122 us -> 110 us
    pallas_call x1, Pallas kernels: 122 us -> 110 us  [local(): pl.pallas_call(lambda *refs: kernel(NP, NT, NX, NY, *refs), out_shape=jax...]
where the time goes in v4:
time: 112 us
  Pallas kernels  110 us (98%)
  local copies, waits for them, and re-layouts  1.29 us (1%)
    pallas_call x1, Pallas kernels, local(): pl.pallas_call(lambda *refs: kernel(NP, NT, NX, NY, *refs), out_shape=jax...  110 us

profile of v4, /device:TPU:1, one launch (start us, length us, event | category | flops | bytes accessed | tf_op | source)
XLA Modules:
  0.0 111.5 jit_solution(7732596553948084771)
XLA Ops:
  0.0 110.2 %shard_map.127 = bf16[8,288]{1,0:T(8,128)(2,1)} custom-call(bf16[8,288]{1,0:T(8,128)(2,1)} %refs_0_.1, bf16[4608,256]{1,0:T(8,128)(2,1)} %refs_1_.1, f32[256]{0:T(256)} %refs_2_.1, s32[64,256]{1,0:T(8,128)} %bitcast.5, bf16[288,4096]{1,0:T(8,128)(2,1)} %bitcast.3, f32[288]{0:T(512)} %refs_5_.1, s32[256]{0:T(256)} %refs_6_.1, f32[4608]{0:T(1024)} %refs_7_.1, ...), custom_call_target="tpu_custom_call" | custom-call | tf_op jit(solution)/shard_map/pallas_call | solution.py:434
  110.3 1.3 %copy.15 = bf16[8,288]{1,0:T(8,128)(2,1)} copy(bf16[8,288]{1,0:T(8,128)(2,1)} %shard_map.127) | data formatting | bytes 9216

commit v5 on v4

--- a/solution.py
+++ b/solution.py
@@ -265,7 +265,7 @@
 
     sub = lax.broadcasted_iota(jnp.int32, (8, 128), 0)
     lft = lax.broadcasted_iota(jnp.int32, (8, 128), 1) < 64
-    @pl.loop(0, NP, unroll=4)
+    @pl.loop(0, NP, unroll=8 if NP % 8 == 0 else 1)
     def _(b):
         relb = IDP[pl.ds(pl.multiple_of(b * 8, 8), 8), :] - g * (NT * 256)
         vb = VG[b].astype(F32)
@@ -369,7 +369,7 @@
     oc.start()
     drains.append(oc.wait_send)
     oc.wait_recv()
-    OSS[...] = OSD[c] + OSR[...]
+    OSS[...] = (OSD[c] + OSR[...]).astype(BF16)
     own = (c == zh) & (s // NH == zh)
     for j in range(NH):
         here = (c == zh) & (zh * NH + j == s)
@@ -393,7 +393,7 @@
             bulk(ref, NZ, sem)
     drains.append(lambda: bulk_own(OSS, ssem.at[14]))
     bulk_own(OR, rsem.at[14])
-    att = jnp.sum(OR[...], axis=0)
+    att = jnp.sum(OR[...].astype(F32), axis=0)
     diag = lax.broadcasted_iota(jnp.int32, (8, 128), 0) == lax.broadcasted_iota(jnp.int32, (8, 128), 1)
     NR[s] = jnp.sum(jnp.where(diag, jnp.sum(att * att, axis=1, keepdims=True), 0.0), axis=0, keepdims=True)
     to_tensor(15, lambda q: NR.at[s], NR.at[s], NR)
@@ -423,7 +423,7 @@
         V((2, 8, CH), F32), V((NT, 16, CH), BF16), V((NT, CH), F32), V((NT, CH), F32),
         V((16, 256), F32), V((16, 256), F32), V((16, 256), F32), V((16, 256), F32), V((16, 256), BF16), V((NP, 16, 256), BF16),
         V((T, 128), F32), V((16, 256), BF16),
-        V((2, NZ, 8, CH), F32), V((NZ, 8, CH), F32), V((NZ, 8, CH), F32), V((NZ, 8, CH), F32),
+        V((2, NZ, 8, CH), F32), V((NZ, 8, CH), F32), V((NZ, 8, CH), BF16), V((NZ, 8, CH), BF16),
         V((NT, 1, 128), F32),
         pltpu.SemaphoreType.DMA((2 * NZ + 5,)), pltpu.SemaphoreType.DMA((26,)),
         pltpu.SemaphoreType.DMA((26,)), pltpu.SemaphoreType.DMA((NX,)), pltpu.SemaphoreType.DMA((NY,)),

time: 112 us -> 110 us (0.982)
  Pallas kernels: 110 us -> 108 us
    pallas_call x1, Pallas kernels: 110 us -> 108 us  [local(): pl.pallas_call(lambda *refs: kernel(NP, NT, NX, NY, *refs), out_shape=jax...]
where the time goes in v5:
time: 110 us; the launch traced here: 109 us
  Pallas kernels  108 us (98%)
  local copies, waits for them, and re-layouts  1.29 us (1%)
    pallas_call x1, Pallas kernels, local(): pl.pallas_call(lambda *refs: kernel(NP, NT, NX, NY, *refs), out_shape=jax...  108 us

profile of v5, /device:TPU:1, one launch (start us, length us, event | category | flops | bytes accessed | tf_op | source)
XLA Modules:
  0.0 109.4 jit_solution(17663970997957526325)
XLA Ops:
  0.0 108.1 %shard_map.127 = bf16[8,288]{1,0:T(8,128)(2,1)} custom-call(bf16[8,288]{1,0:T(8,128)(2,1)} %refs_0_.1, bf16[4608,256]{1,0:T(8,128)(2,1)} %refs_1_.1, f32[256]{0:T(256)} %refs_2_.1, s32[64,256]{1,0:T(8,128)} %bitcast.5, bf16[288,4096]{1,0:T(8,128)(2,1)} %bitcast.3, f32[288]{0:T(512)} %refs_5_.1, s32[256]{0:T(256)} %refs_6_.1, f32[4608]{0:T(1024)} %refs_7_.1, ...), custom_call_target="tpu_custom_call" | custom-call | tf_op jit(solution)/shard_map/pallas_call | solution.py:434
  108.1 1.3 %copy.15 = bf16[8,288]{1,0:T(8,128)(2,1)} copy(bf16[8,288]{1,0:T(8,128)(2,1)} %shard_map.127) | data formatting | bytes 9216

commit v6 on v5

--- a/solution.py
+++ b/solution.py
@@ -199,8 +199,8 @@
             land(col_b, r2x.at[xx])
             on(slice(None), xx, slice(None), Bh)
     drains.append(lambda: land(X.at[0], ssem.at[2]))
+    to_y(9, own_k, own_k, own_ks)
     to_x(8, own_q, own_q, own_qs)
-    to_y(9, own_k, own_k, own_ks)
     to_x(16, own_ba, own_ba, own_bas)
     to_y(20, own_bb, own_bb, own_bbs)
 
@@ -233,10 +233,10 @@
         @pl.when(s != first + k)
         def _():
             rcopy(VS.at[pl.ds(k * NB, NB)], VR.at[s], 3, g, first + k).start()
+    land(own_ks, rsem.at[9])
+    to_x(22, col_k, col_k, col_ks)
     land(own_qs, rsem.at[8])
     to_y(21, row_q, row_q, row_qs)
-    land(own_ks, rsem.at[9])
-    to_x(22, col_k, col_k, col_ks)
 
     @pl.when(middle)
     def _():

time: 110 us -> 110 us (level)
  no operation moved by 1% of the time
where the time goes in v6:
time: 110 us; the launch traced here: 109 us
  Pallas kernels  108 us (98%)
  local copies, waits for them, and re-layouts  1.29 us (1%)
    pallas_call x1, Pallas kernels, local(): pl.pallas_call(lambda *refs: kernel(NP, NT, NX, NY, *refs), out_shape=jax...  108 us

profile of v6, /device:TPU:1, one launch (start us, length us, event | category | flops | bytes accessed | tf_op | source)
XLA Modules:
  0.0 109.3 jit_solution(904956076668696920)
XLA Ops:
  0.0 108.0 %shard_map.127 = bf16[8,288]{1,0:T(8,128)(2,1)} custom-call(bf16[8,288]{1,0:T(8,128)(2,1)} %refs_0_.1, bf16[4608,256]{1,0:T(8,128)(2,1)} %refs_1_.1, f32[256]{0:T(256)} %refs_2_.1, s32[64,256]{1,0:T(8,128)} %bitcast.5, bf16[288,4096]{1,0:T(8,128)(2,1)} %bitcast.3, f32[288]{0:T(512)} %refs_5_.1, s32[256]{0:T(256)} %refs_6_.1, f32[4608]{0:T(1024)} %refs_7_.1, ...), custom_call_target="tpu_custom_call" | custom-call | tf_op jit(solution)/shard_map/pallas_call | solution.py:434
  108.0 1.3 %copy.15 = bf16[8,288]{1,0:T(8,128)(2,1)} copy(bf16[8,288]{1,0:T(8,128)(2,1)} %shard_map.127) | data formatting | bytes 9216
